TPU v7x, 32 devices: a whole 2x2x4 slice. The times are simulated.
32 devices in a mesh: blk: 8 (over z, x), feat: 4 (over y, core).
Axes of the slice: x: 2, y: 2, z: 4, core: 2. Of those that a mesh axis runs over, the one named last changes fastest.
Arguments:
- features: bfloat16 [8192, 512], P(('blk', 'feat')), may hold values from -8 to 8
- weight: bfloat16 [512, 512], replicated, may hold values from -0.25 to 0.25
- tile_vals: bfloat16 [8, 160, 128, 128], P('blk'), may hold values from 0 to 3, as said below
- pair_counts: int32 [8, 8], P('blk'), may hold values from 0 to 20, as said below
- slot_row: int32 [8, 160], P('blk'), may hold values from 0 to 7
- slot_col: int32 [8, 160], P('blk'), may hold values from 0 to 7
- cotangent: bfloat16 [8192, 512], P('blk', 'feat'), may hold values from -6 to 6
Outputs:
- output: bfloat16 [8192, 512], P('blk', 'feat')
- grad_features: bfloat16 [8192, 512], P(('blk', 'feat'))
- grad_weight: float32 [512, 512], P(None, 'feat')
Inputs may be any that keep to these rules, and one draw needn't show every extreme that they name: `pair_counts`: each row block's counts lie between half of a limit drawn for that row block and the limit; every pair (b, b) holds 20 filled slots. `tile_vals`: entries are zero or positive edge weights.
All inputs are finite; a program needn't handle non-finite values.
Results may differ from a plain program's by a relative error of at most 0.018.
Values may be sent and summed in bfloat16 or wider, within the bound.
A program may use at most 128 MiB of HBM per device.

v0:
```python
import jax
import jax.numpy as jnp
from jax import lax
from jax.sharding import PartitionSpec as P


def activation(values):
    return jax.nn.gelu(values, approximate=True)


def per_device(features, weight, tile_vals, pair_counts, slot_row, slot_col, cotangent):
    tiles = tile_vals[0]
    counts = pair_counts[0]
    row_ids = slot_row[0]
    col_ids = slot_col[0]
    tile_size = tiles.shape[1]
    blocks = lax.axis_size("blk")
    slots = tiles.shape[0]
    capacity = slots // blocks
    rows_dev = cotangent.shape[0]
    columns = cotangent.shape[1]
    tiles_row = rows_dev // tile_size
    quarter = features.shape[0]
    node_total = rows_dev * blocks
    my_feat = lax.axis_index("feat")
    filled_all = (jnp.arange(slots) % capacity < jnp.repeat(counts, capacity)).astype(jnp.float32)
    placing_all = (row_ids[None, :] == jnp.arange(tiles_row)[:, None]).astype(
        jnp.float32
    ) * filled_all[None, :]
    row_sums = jnp.einsum(
        "sij,j->si", tiles, jnp.ones((tile_size,), jnp.bfloat16), preferred_element_type=jnp.float32
    )
    degree = 1.0 + jnp.einsum("rs,si->ri", placing_all, row_sums, precision=lax.Precision.HIGHEST)
    scaling = lax.rsqrt(degree).reshape(rows_dev)

    def pair_slots(column):
        first = column * capacity
        chosen = lax.dynamic_slice_in_dim(tiles, first, capacity, 0)
        rows_here = lax.dynamic_slice_in_dim(row_ids, first, capacity, 0)
        cols_here = lax.dynamic_slice_in_dim(col_ids, first, capacity, 0)
        filled = (jnp.arange(capacity) < lax.dynamic_slice_in_dim(counts, column, 1, 0)).astype(
            jnp.float32
        )
        return (chosen, rows_here, cols_here, filled)

    def forward_part(block, column):
        chosen, rows_here, cols_here, filled = pair_slots(column)
        picking = (cols_here[:, None] == jnp.arange(tiles_row)[None, :]).astype(jnp.bfloat16)
        picked = jnp.einsum(
            "sr,rjf->sjf",
            picking,
            block.reshape(tiles_row, tile_size, columns),
            preferred_element_type=jnp.float32,
        ).astype(jnp.bfloat16)
        product = jnp.einsum("sij,sjf->sif", chosen, picked, preferred_element_type=jnp.float32)
        placing = (rows_here[None, :] == jnp.arange(tiles_row)[:, None]).astype(
            jnp.float32
        ) * filled[None, :]
        return jnp.einsum("rs,sif->rif", placing, product, precision=lax.Precision.HIGHEST).reshape(
            rows_dev, columns
        )

    def backward_part(grads, column):
        chosen, rows_here, cols_here, filled = pair_slots(column)
        picking = (rows_here[:, None] == jnp.arange(tiles_row)[None, :]).astype(jnp.bfloat16)
        picked = jnp.einsum(
            "sr,rif->sif",
            picking,
            grads.reshape(tiles_row, tile_size, columns),
            preferred_element_type=jnp.float32,
        ).astype(jnp.bfloat16)
        product = jnp.einsum("sij,sif->sjf", chosen, picked, preferred_element_type=jnp.float32)
        placing = (cols_here[None, :] == jnp.arange(tiles_row)[:, None]).astype(
            jnp.float32
        ) * filled[None, :]
        return jnp.einsum("rs,sjf->rjf", placing, product, precision=lax.Precision.HIGHEST).reshape(
            rows_dev, columns
        )

    scaling_rows = lax.dynamic_slice_in_dim(scaling, my_feat * quarter, quarter, 0)
    hidden = jnp.dot(features, weight, preferred_element_type=jnp.float32)
    local_rows = (scaling_rows[:, None] * hidden).astype(jnp.bfloat16)
    scaled = lax.all_to_all(local_rows, "feat", split_axis=1, concat_axis=0, tiled=True)
    shard_rows = lax.all_gather(scaled, "blk", axis=0, tiled=True)
    number = shard_rows.shape[0] // rows_dev

    def fold_visit(ordinal, partial_sum):
        block = lax.dynamic_slice_in_dim(shard_rows, ordinal * rows_dev, rows_dev, 0)
        return partial_sum + forward_part(block, ordinal)

    gathered_sum = lax.fori_loop(0, number, fold_visit, jnp.zeros((rows_dev, columns), jnp.float32))
    preact = scaling[:, None] * (gathered_sum + scaled.astype(jnp.float32))
    output = activation(preact).astype(jnp.bfloat16)
    grad_preact = jax.vjp(activation, preact)[1](cotangent.astype(jnp.float32))[0]
    scaled_grad = (scaling[:, None] * grad_preact).astype(jnp.bfloat16)

    def column_visit(ordinal, terms):
        return lax.dynamic_update_slice_in_dim(
            terms, backward_part(scaled_grad, ordinal), ordinal * rows_dev, 0
        )

    back_sums = lax.psum_scatter(
        lax.fori_loop(
            0,
            rows_dev * lax.axis_size("blk") // rows_dev,
            column_visit,
            jnp.zeros((rows_dev * lax.axis_size("blk"), columns), jnp.float32),
        ).astype(jnp.bfloat16),
        "blk",
        scatter_dimension=0,
        tiled=True,
    ).astype(jnp.float32)
    hidden_grad = (scaling[:, None] * (back_sums + scaled_grad.astype(jnp.float32))).astype(
        jnp.bfloat16
    )
    grad_local = lax.all_to_all(hidden_grad, "feat", split_axis=0, concat_axis=1, tiled=True)
    partial_grad = lax.dot_general(
        features, grad_local, (((0,), (0,)), ((), ())), preferred_element_type=jnp.float32
    )
    summed_rows = lax.psum(partial_grad.astype(jnp.bfloat16), "blk")
    weight_grad = lax.psum_scatter(summed_rows, "feat", scatter_dimension=1, tiled=True).astype(
        jnp.float32
    )
    grad_features = lax.dot_general(
        grad_local, weight, (((1,), (1,)), ((), ())), preferred_element_type=jnp.float32
    ).astype(jnp.bfloat16)
    grad_weight = weight_grad * node_total ** (-0.5)
    return (output, grad_features, grad_weight)


def solution(mesh):
    in_specs = (
        P(("blk", "feat"), None),
        P(),
        P("blk", None, None, None),
        P("blk", None),
        P("blk", None),
        P("blk", None),
        P("blk", "feat"),
    )
    out_specs = (P("blk", "feat"), P(("blk", "feat"), None), P(None, "feat"))
    return jax.shard_map(
        per_device, mesh=mesh, in_specs=in_specs, out_specs=out_specs, check_vma=False
    )
```

profile of v0, /device:TPU:0, one launch (start us, length us, event | category | flops | bytes accessed | tf_op | source)
XLA Modules:
  0.0 344.9 jit_solution(6193988609464363884)
XLA Ops:
  7.2 0.8 broadcast_in_dim.45
  8.1 4.0 %fusion.52 = f32[1,160,128]{2,0,1:T(1,128)S(1)} fusion(bf16[1,160,128,128]{3,2,1,0:T(8,128)(2,1)} %param.13), kind=kOutput, calls=%fused_computation.77 | convolution fusion | flops 5242880 | bytes 5324800 | tf_op jit(solution)/shard_map/sij,j->si/dot_general | solution.py:30
  12.8 10.2 %all_to_all.38 = bf16[256,4,128]{2,0,1:T(8,128)(2,1)} all-to-all(bf16[256,4,128]{2,0,1:T(8,128)(2,1)S(1)} %bitcast.79), channel_id=1, replica_groups=mesh['blk'=8,'feat'=4] {'feat'}, dimensions={1} | all-to-all | bytes 524288 | tf_op jit(solution)/shard_map/all_to_all | solution.py:83
  23.0 50.0 %all-gather.2.cloned.1.call-done = bf16[8192,128]{1,0:T(8,128)(2,1)} async-done(((bf16[1024,128]{1,0:T(8,128)(2,1)}), bf16[8192,128]{1,0:T(8,128)(2,1)}) %all-gather.2.cloned.1.call-update) | async-done | bytes 2097168 | tf_op jit(solution)/shard_map/all_gather | solution.py:84
  73.1 49.1 %while.28 = (s32[]{:T(128)}, f32[1024,128]{1,0:T(8,128)S(1)}, s32[160]{0:T(256)S(1)}, s32[8]{0:T(128)S(1)}, bf16[160,128,128]{2,1,0:T(8,128)(2,1)}, /*index=5*/s...) while((s32[]{:T(128)}, f32[1024,128]{1,0:T(8,128)S(1)}, ...), condition=%wide.region_1.2_spmd.clone, body=%wide.region_0.1_spmd.clone.sunk | while | flops 121176592 | bytes 8520579 | solution.py:91
  73.2 1.0 constant_dynamic-slice_fusion.2
  74.6 1.4 fusion.94
  76.7 0.6 compare_convert_fusion.6
  77.4 1.7 fusion.95
  79.4 1.0 constant_dynamic-slice_fusion.2
  80.8 1.4 fusion.94
  82.8 0.6 compare_convert_fusion.6
  83.5 1.7 fusion.95
  85.5 1.0 constant_dynamic-slice_fusion.2
  86.9 1.4 fusion.94
  89.0 0.6 compare_convert_fusion.6
  89.6 1.7 fusion.95
  91.6 1.0 constant_dynamic-slice_fusion.2
  93.0 1.4 fusion.94
  95.1 0.6 compare_convert_fusion.6
  95.8 1.7 fusion.95
  97.7 1.0 constant_dynamic-slice_fusion.2
  99.1 1.4 fusion.94
  101.2 0.6 compare_convert_fusion.6
  101.9 1.7 fusion.95
  103.9 1.0 constant_dynamic-slice_fusion.2
  105.3 1.4 fusion.94
  107.4 0.6 compare_convert_fusion.6
  108.0 1.7 fusion.95
  110.0 1.0 constant_dynamic-slice_fusion.2
  111.4 1.4 fusion.94
  114.1 1.7 fusion.95
  116.1 1.0 constant_dynamic-slice_fusion.2
  117.5 1.4 fusion.94
  120.3 1.7 fusion.95
  122.2 1.3 fusion.40
  123.7 40.8 %while.27 = (s32[]{:T(128)}, bf16[8192,128]{1,0:T(8,128)(2,1)S(1)}, s32[160]{0:T(256)S(1)}, s32[8]{0:T(128)S(1)}, bf16[160,128,128]{2,1,0:T(8,128)(2,1)}, /*inde...) while((s32[]{:T(128)}, bf16[8192,128]{1,0:T(8,128)(2,1)S(1)}, ...), condition=%wide.region_3.4_spmd, body=%wide.region_2.3_spmd.sunk | while | flops 120914448 | bytes 6161273 | solution.py:103
  124.3 1.5 fusion.86
  127.1 1.7 fusion.87
  129.4 1.5 fusion.86
  132.2 1.7 fusion.87
  134.5 1.5 fusion.86
  136.6 0.6 compare_convert_fusion.5
  137.3 1.7 fusion.87
  139.6 1.5 fusion.86
  142.4 1.7 fusion.87
  144.7 1.5 fusion.86
  147.5 1.7 fusion.87
  149.8 1.5 fusion.86
  152.6 1.7 fusion.87
  154.9 1.5 fusion.86
  157.7 1.7 fusion.87
  160.0 1.5 fusion.86
  162.8 1.7 fusion.87
  164.6 1.3 copy-done.1
  166.0 66.4 %reduce-scatter.3.cloned.1.call-done = bf16[1024,128]{1,0:T(8,128)(2,1)} async-done(((bf16[8192,128]{1,0:T(8,128)(2,1)}), bf16[1024,128]{1,0:T(8,128)(2,1)}) %reduce-scatter.3.cloned.1.call-update) | async-done | bytes 262160 | tf_op jit(solution)/shard_map/reduce_scatter | solution.py:102
  232.4 1.1 multiply_convert_fusion
  233.5 8.6 %all_to_all.39 = bf16[4,256,128]{2,1,0:T(8,128)(2,1)S(1)} all-to-all(bf16[4,256,128]{2,1,0:T(8,128)(2,1)S(1)} %bitcast.78), channel_id=1, replica_groups=mesh['blk'=8,'feat'=4] {'feat'}, dimensions={0} | all-to-all | bytes 524288 | tf_op jit(solution)/shard_map/all_to_all | solution.py:116
  242.3 1.1 fusion.32
  243.4 19.8 %reduce-scatter.5.cloned.1.call-done = bf16[512,128]{0,1:T(8,128)(2,1)} async-done(((bf16[512,512]{0,1:T(8,128)(2,1)}), bf16[512,128]{0,1:T(8,128)(2,1)}) %reduce-scatter.5.cloned.1.call-update) | async-done | bytes 131088 | tf_op jit(solution)/shard_map/reduce_scatter | solution.py:121
  263.3 1.1 convolution_convert_fusion.3
  264.4 72.3 %all-reduce.2.cloned.1.call-done = bf16[512,128]{0,1:T(8,128)(2,1)} async-done(((bf16[512,128]{0,1:T(8,128)(2,1)}), bf16[512,128]{0,1:T(8,128)(2,1)}) %all-reduce.2.cloned.1.call-update) | async-done | bytes 131088 | tf_op jit(solution)/shard_map/psum | solution.py:120
  336.6 0.9 convert_multiply_fusion.2
  337.5 0.8 copy.50
  (137 shorter events, 28.0 us)
Async XLA Ops:
  7.2 5.2 %copy-start = (bf16[512,512]{1,0:T(8,128)(2,1)S(1)}, bf16[512,512]{1,0:T(8,128)(2,1)}, u32[]{:S(2)}) copy-start(bf16[512,512]{1,0:T(8,128)(2,1)} %param.12) | copy-start | bytes 1572868
  7.2 65.9 %all-gather.2.cloned.1.call-start = ((), (), s32[]{:S(2)}) async-start(), calls=%async_computation.4 | async-start | bytes 2359296 | tf_op jit(solution)/shard_map/all_gather | solution.py:84
  8.1 4.0 %copy-start.5 = (s32[1,160]{1,0:T(1,128)S(1)}, s32[1,160]{1,0:T(1,128)}, u32[]{:S(2)}) copy-start(s32[1,160]{1,0:T(1,128)} %param.15) | copy-start | bytes 1924
  8.1 4.3 %copy-start.3 = (bf16[256,512]{1,0:T(8,128)(2,1)S(1)}, bf16[256,512]{1,0:T(8,128)(2,1)}, u32[]{:S(2)}) copy-start(bf16[256,512]{1,0:T(8,128)(2,1)} %param.11) | copy-start | bytes 786436
  12.1 61.0 %copy-start.6 = (s32[1,8]{1,0:T(1,128)S(1)}, s32[1,8]{1,0:T(1,128)}, u32[]{:S(2)}) copy-start(s32[1,8]{1,0:T(1,128)} %param.14) | copy-start | bytes 100
  12.1 61.0 %copy-start.7 = (s32[1,160]{1,0:T(1,128)S(1)}, s32[1,160]{1,0:T(1,128)}, u32[]{:S(2)}) copy-start(s32[1,160]{1,0:T(1,128)} %param.16) | copy-start | bytes 1924
  23.0 209.4 %reduce-scatter.3.cloned.1.call-start = ((), (), s32[]{:S(2)}) async-start(), calls=%async_computation.5 | async-start | bytes 2359296 | tf_op jit(solution)/shard_map/reduce_scatter | solution.py:102
  73.1 49.1 %copy-start.2 = (bf16[256,4,128]{2,0,1:T(8,128)(2,1)S(1)}, bf16[256,4,128]{2,0,1:T(8,128)(2,1)}, u32[]{:S(2)}) copy-start(bf16[256,4,128]{2,0,1:T(8,128)(2,1)} %all_to_all.38) | copy-start | bytes 786436
  73.1 49.1 %copy-start.4 = (bf16[1024,128]{1,0:T(8,128)(2,1)S(1)}, bf16[1024,128]{1,0:T(8,128)(2,1)}, u32[]{:S(2)}) copy-start(bf16[1024,128]{1,0:T(8,128)(2,1)} %param.17) | copy-start | bytes 786436
  164.6 1.3 copy-start.1
  165.9 97.3 %reduce-scatter.5.cloned.1.call-start = ((), (), s32[]{:S(2)}) async-start(), calls=%async_computation.6 | async-start | bytes 655360 | tf_op jit(solution)/shard_map/reduce_scatter | solution.py:121
  243.4 93.2 %all-reduce.2.cloned.1.call-start = ((), (), s32[]{:S(2)}) async-start(), calls=%async_computation.7 | async-start | bytes 262144 | tf_op jit(solution)/shard_map/psum | solution.py:120
Sparse Core Ops, SparseCore 0:
  23.1 49.9 all-gather.1
  166.0 66.2 reduce-scatter.2
  243.5 19.7 reduce-scatter.4
  266.8 69.7 all-reduce.1
where the time goes:
time: 346 us; the launch traced here: 345 us
  waiting for transfers between devices  209 us (60%)
  matrix products  63.1 us (18%)
  local copies, waits for them, and re-layouts  24.7 us (7%)
  blocking collectives  18.8 us (5%)
  other arithmetic  14.5 us (4%)
  between operations  13.9 us (4%)
    psum x1, waiting for transfers between devices, per_device(): summed_rows = lax.psum(partial_grad.astype(jnp.bfloat16), 'blk')  72.3 us
    reduce_scatter x1, waiting for transfers between devices, per_device(): lax.psum_scatter(lax.fori_loop(0, rows_dev * lax.axis_size('blk') // rows...  66.4 us
    all_gather x1, waiting for transfers between devices, per_device(): shard_rows = lax.all_gather(scaled, 'blk', axis=0, tiled=True)  50 us
    reduce_scatter x1, waiting for transfers between devices, per_device(): lax.psum_scatter(summed_rows, 'feat', scatter_dimension=1, tiled=True)  19.8 us
    dot_general x8, matrix products, backward_part(): jnp.einsum('rs,sjf->rjf', placing, product, precision=lax.Precision.HIGHEST)  13.3 us
    dot_general x8, matrix products, forward_part(): jnp.einsum('rs,sif->rif', placing, product, precision=lax.Precision.HIGHEST)  13.3 us
    dot_general x8, matrix products, backward_part(): jnp.einsum('sij,sif->sjf', chosen, picked, preferred_element_type=jnp.flo...  11.9 us
    dot_general x8, matrix products, forward_part(): jnp.einsum('sij,sjf->sif', chosen, picked, preferred_element_type=jnp.flo...  11.4 us
  transfers between devices with their start and end apart: 4, of which 4 were waited for; matrix products, arithmetic and copies ran while one was open for 0% of the time, Pallas kernels for 0%

commit v1 on v0

v1 whole, which is shorter than its diff:
```python
import functools

import jax
import jax.numpy as jnp
from jax import lax
from jax.experimental import pallas as pl
from jax.experimental.pallas import tpu as pltpu
from jax.sharding import PartitionSpec as P

MESH = pl.DeviceIdType.MESH
VMEM = pl.BlockSpec(memory_space=pltpu.VMEM)
F32, BF16 = jnp.float32, jnp.bfloat16
LIMIT = 56 * 1024 * 1024
CUTS = 2
GELU_C = 0.7978845608028654
GELU_A = 0.044715


def ring_of(n):
    me = lax.axis_index("blk")
    half = n // 2
    pos = jnp.where(me % 2 == 0, me // 2, n - 1 - me // 2)

    def blk_of(p):
        p = (p + 2 * n) % n
        return jnp.where(p < half, 2 * p, 2 * (n - 1 - p) + 1)

    return me, pos, blk_of


def greet(peers):
    barrier = pltpu.get_barrier_semaphore()
    for peer in peers:
        pl.semaphore_signal(barrier, inc=1, device_id=peer, device_id_type=MESH)
    pl.semaphore_wait(barrier, len(peers))


def remote(src, dst, send, recv, peer):
    return pltpu.make_async_remote_copy(
        src_ref=src, dst_ref=dst, send_sem=send, recv_sem=recv, device_id=peer, device_id_type=MESH
    )


def scaling_kernel(steps, per, tiles_row, rows_ref, tiles_ref, sc_ref, sct_ref, acc):
    step = pl.program_id(0)

    @pl.when(step == 0)
    def _():
        acc[...] = jnp.zeros_like(acc)

    for k in range(per):
        acc[rows_ref[step * per + k]] += tiles_ref[k].astype(F32)

    @pl.when(step == steps - 1)
    def _():
        for t in range(tiles_row):
            degree = 1.0 + jnp.sum(acc[t], axis=1, keepdims=True)
            wide = jnp.broadcast_to(lax.rsqrt(degree), acc.shape[1:])
            sc_ref[t] = wide
            sct_ref[t] = wide.T[0:8]


def gather_kernel(n, nf, feat_ref, w_ref, sc_ref, all_ref, fb_ref, buf, as_, ar, fs, fr, rs, rr):
    me, pos, blk_of = ring_of(n)
    mf = lax.axis_index("feat")
    quarter = feat_ref.shape[0]
    cols = all_ref.shape[2]
    right, left = (blk_of(pos + 1), mf), (blk_of(pos - 1), mf)
    peers = [(me, (mf + d) % nf) for d in range(1, nf)]
    greet(peers + [right, left])
    mine = pl.ds(pl.multiple_of(mf * quarter, quarter), quarter)
    scale = sc_ref[mine, :]

    def rows_for(f):
        w = w_ref[:, pl.ds(pl.multiple_of(f * cols, cols), cols)]
        h = jnp.dot(feat_ref[...], w, preferred_element_type=F32)
        return (scale * h).astype(BF16)

    first = []
    for d in (2, 3, 1):
        peer = peers[d - 1]
        buf[d - 1] = rows_for(peer[1])
        copy = remote(buf.at[d - 1], all_ref.at[me, mine], as_.at[d - 1], ar.at[d - 1], peer)
        copy.start()
        first.append(copy)
    all_ref[me, mine, :] = rows_for(mf)
    fb_ref[mine, :] = feat_ref[...]
    for copy in first:
        copy.wait_recv()

    rows = all_ref.shape[1]
    chunk = rows // (2 * CUTS)

    def step_copy(d, s, q):
        block = blk_of(pos - s) if d == 0 else blk_of(pos + s)
        part = all_ref.at[block, pl.ds((d * CUTS + q) * chunk, chunk)]
        return remote(part, part, rs.at[d, s, q], rr.at[d, s, q], right if d == 0 else left)

    for q in range(CUTS):
        for d in range(2):
            step_copy(d, 0, q).start()
    later = []
    for d in range(1, nf):
        copy = remote(feat_ref, fb_ref.at[mine], fs.at[d - 1], fr.at[d - 1], peers[d - 1])
        copy.start()
        later.append(copy)

    def step(s, carry):
        for q in range(CUTS):
            for d in range(2):
                step_copy(d, s - 1, q).wait_recv()
                step_copy(d, s, q).start()
        return carry

    lax.fori_loop(1, n - 1, step, 0)
    for q in range(CUTS):
        for d in range(2):
            step_copy(d, n - 2, q).wait_recv()

    def drain(s, carry):
        for q in range(CUTS):
            for d in range(2):
                step_copy(d, s, q).wait_send()
        return carry

    lax.fori_loop(0, n - 1, drain, 0)
    for copy in later:
        copy.wait_recv()
    for copy in first + later:
        copy.wait_send()


def product_kernel(
    n, cap, tiles_row, idx, where, s_ref, own_ref, tiles_ref, sc_ref, cot_ref, out_ref, terms_ref, acc, gt
):
    step = pl.program_id(0)
    c = step % n
    first = c * cap
    tile = tiles_ref.shape[1]

    @pl.when((step == 0) | (step >= n))
    def _():
        acc[...] = jnp.zeros_like(acc)

    @pl.when(step < n)
    def _():
        for k in range(cap):
            col = pl.multiple_of(idx[2, first + k] * tile, tile)
            acc[idx[1, first + k]] += jnp.dot(
                tiles_ref[k], s_ref[0, pl.ds(col, tile), :], preferred_element_type=F32
            )

    @pl.when(step == n - 1)
    def _():
        for t in range(tiles_row):
            part = pl.ds(t * tile, tile)
            scale = sc_ref[part, :]
            v = scale * (acc[t] + own_ref[0, part, :].astype(F32))
            square = v * v
            th = jnp.tanh(GELU_C * (v + GELU_A * (square * v)))
            half = 0.5 * (1.0 + th)
            out_ref[part, :] = (v * half).astype(BF16)
            slope = half + 0.5 * v * (1.0 - th * th) * (GELU_C * (1.0 + 3.0 * GELU_A * square))
            grad = scale * (slope * cot_ref[part, :].astype(F32))
            gt[t] = grad.T.astype(BF16)

    @pl.when(step >= n)
    def _():
        for k in range(cap):
            acc[idx[3, first + k]] += jnp.dot(
                gt[idx[0, first + k]], tiles_ref[k], preferred_element_type=F32
            )
        own = jnp.where(c == where[0], 1.0, 0.0)
        for t in range(tiles_row):
            terms_ref[0, pl.ds(t * tile, tile), :] = (acc[t] + own * gt[t].astype(F32)).astype(BF16)


def scatter_kernel(
    n, nf, tile, factor, terms_ref, sct_ref, fb_ref, w_ref, gf_ref, gw_ref,
    land, hgt, hg, hg4, wbuf, wland, wsum, wfin, rs, rr, as_, ar, ws, wr, vs, vr,
):
    me, pos, blk_of = ring_of(n)
    mf = lax.axis_index("feat")
    right, left = (blk_of(pos + 1), mf), (blk_of(pos - 1), mf)
    fpeers = [(me, (mf + d) % nf) for d in range(1, nf)]
    bpeers = [((me + d) % n, mf) for d in range(1, n)]
    greet(fpeers + bpeers)
    rows = terms_ref.shape[1]
    chunk = rows // (2 * CUTS)

    def own_part(d, s, q):
        block = blk_of(pos - 1 - s) if d == 0 else blk_of(pos + 1 + s)
        return block, pl.ds((d * CUTS + q) * chunk, chunk)

    def step_copy(src, d, s, q):
        return remote(src, land.at[d, s, q], rs.at[d, s, q], rr.at[d, s, q], right if d == 0 else left)

    for q in range(CUTS):
        for d in range(2):
            step_copy(terms_ref.at[own_part(d, 0, q)], d, 0, q).start()

    def step(s, carry):
        for q in range(CUTS):
            for d in range(2):
                step_copy(land.at[d, s - 1, q], d, s - 1, q).wait_recv()
                block, part = own_part(d, s, q)
                summed = land[d, s - 1, q].astype(F32) + terms_ref[block, part, :].astype(F32)
                land[d, s - 1, q] = summed.astype(BF16)
                step_copy(land.at[d, s - 1, q], d, s, q).start()
        return carry

    lax.fori_loop(1, n - 1, step, 0)
    for q in range(CUTS):
        for d in range(2):
            step_copy(land.at[d, n - 2, q], d, n - 2, q).wait_recv()
            for t in range(chunk // tile):
                at = (d * CUTS + q) * chunk + t * tile
                total = land[d, n - 2, q, t * tile:(t + 1) * tile, :].astype(F32) + terms_ref[
                    me, at:at + tile, :
                ].astype(F32)
                total = total * sct_ref[at // tile][0:1, :]
                hgt[:, at:at + tile] = total.astype(BF16)
                hg[at:at + tile, :] = total.T.astype(BF16)

    quarter = rows // nf
    sent = []
    for d in (2, 3, 1):
        peer = fpeers[d - 1]
        src = hg.at[pl.ds(pl.multiple_of(peer[1] * quarter, quarter), quarter)]
        copy = remote(src, hg4.at[mf], as_.at[d - 1], ar.at[d - 1], peer)
        copy.start()
        sent.append(copy)
    hg4[mf] = hg[pl.ds(pl.multiple_of(mf * quarter, quarter), quarter), :]

    wgt = jnp.dot(hgt[...], fb_ref[...], preferred_element_type=F32)
    wbuf[...] = wgt.T.astype(BF16)
    piece = wsum.shape[0]

    def piece_of(b):
        return pl.ds(pl.multiple_of(b * piece, piece), piece)

    pieces = []
    for d in range(1, n):
        peer = bpeers[d - 1]
        copy = remote(wbuf.at[piece_of(peer[0])], wland.at[d - 1], ws.at[d - 1], wr.at[d - 1], peer)
        copy.start()
        pieces.append(copy)
    for copy in sent:
        copy.wait_recv()
    cols = hg.shape[1]
    total = None
    for f in range(nf):
        part = lax.dot_general(
            hg4[f], w_ref[:, f * cols:(f + 1) * cols], (((1,), (1,)), ((), ())),
            preferred_element_type=F32,
        )
        total = part if total is None else total + part
    gf_ref[...] = total.astype(BF16)
    summed = wbuf[piece_of(me), :].astype(F32)
    for d in range(1, n):
        pieces[d - 1].wait_recv()
        summed = summed + wland[d - 1].astype(F32)
    wsum[...] = summed.astype(BF16)
    finals = []
    for d in range(1, n):
        copy = remote(wsum, wfin.at[piece_of(me)], vs.at[d - 1], vr.at[d - 1], bpeers[d - 1])
        copy.start()
        finals.append(copy)
    wfin[piece_of(me), :] = wsum[...]

    def drain(s, carry):
        for q in range(CUTS):
            for d in range(2):
                step_copy(land.at[d, s, q], d, s, q).wait_send()
        return carry

    lax.fori_loop(0, n - 1, drain, 0)
    for copy in sent + pieces:
        copy.wait_send()
    for copy in finals:
        copy.wait_recv()
    gw_ref[...] = wfin[...].astype(F32) * factor
    for copy in finals:
        copy.wait_send()


def per_device(features, weight, tile_vals, pair_counts, slot_row, slot_col, cotangent):
    n = lax.axis_size("blk")
    nf = lax.axis_size("feat")
    tiles = tile_vals[0]
    slots, tile, _ = tiles.shape
    cap = slots // n
    rows, cols = cotangent.shape
    quarter, width = features.shape
    tiles_row = rows // tile
    filled = jnp.arange(slots) % cap < jnp.repeat(pair_counts[0], cap)
    row_ids, col_ids = slot_row[0], slot_col[0]
    idx = jnp.stack(
        [row_ids, jnp.where(filled, row_ids, tiles_row), col_ids, jnp.where(filled, col_ids, tiles_row)]
    ).astype(jnp.int32)
    where = jnp.full((1,), lax.axis_index("blk"), jnp.int32)
    dma = pltpu.SemaphoreType.DMA
    local = functools.partial(
        pltpu.CompilerParams, dimension_semantics=("arbitrary",), vmem_limit_bytes=LIMIT
    )

    sc, sct = pl.pallas_call(
        functools.partial(scaling_kernel, n, cap, tiles_row),
        grid_spec=pltpu.PrefetchScalarGridSpec(
            num_scalar_prefetch=1,
            grid=(n,),
            in_specs=[pl.BlockSpec((cap, tile, tile), lambda i, r: (i, 0, 0))],
            out_specs=[
                pl.BlockSpec((tiles_row, tile, tile), lambda i, r: (0, 0, 0)),
                pl.BlockSpec((tiles_row, 8, tile), lambda i, r: (0, 0, 0)),
            ],
            scratch_shapes=[pltpu.VMEM((tiles_row + 1, tile, tile), F32)],
        ),
        out_shape=[
            jax.ShapeDtypeStruct((tiles_row, tile, tile), F32),
            jax.ShapeDtypeStruct((tiles_row, 8, tile), F32),
        ],
        compiler_params=local(),
        name="scaling",
    )(idx[1], tiles)
    sc = sc.reshape(rows, tile)

    gathered, fblock = pl.pallas_call(
        functools.partial(gather_kernel, n, nf),
        out_shape=[
            jax.ShapeDtypeStruct((n, rows, cols), BF16),
            jax.ShapeDtypeStruct((rows, width), BF16),
        ],
        in_specs=[VMEM] * 3,
        out_specs=[VMEM] * 2,
        scratch_shapes=[
            pltpu.VMEM((nf - 1, quarter, cols), BF16),
            dma((nf - 1,)), dma((nf - 1,)), dma((nf - 1,)), dma((nf - 1,)),
            dma((2, n - 1, CUTS)), dma((2, n - 1, CUTS)),
        ],
        compiler_params=pltpu.CompilerParams(
            collective_id=0, has_side_effects=True, vmem_limit_bytes=LIMIT
        ),
        name="gather",
    )(features, weight, sc)

    output, terms = pl.pallas_call(
        functools.partial(product_kernel, n, cap, tiles_row),
        grid_spec=pltpu.PrefetchScalarGridSpec(
            num_scalar_prefetch=2,
            grid=(2 * n,),
            in_specs=[
                pl.BlockSpec((1, rows, cols), lambda i, r, w: (jnp.minimum(i, n - 1), 0, 0)),
                pl.BlockSpec((1, rows, cols), lambda i, r, w: (w[0], 0, 0)),
                pl.BlockSpec((cap, tile, tile), lambda i, r, w: (i % n, 0, 0)),
                pl.BlockSpec((rows, cols), lambda i, r, w: (0, 0)),
                pl.BlockSpec((rows, cols), lambda i, r, w: (0, 0)),
            ],
            out_specs=[
                pl.BlockSpec((rows, cols), lambda i, r, w: (0, 0)),
                pl.BlockSpec((1, rows, cols), lambda i, r, w: (jnp.maximum(i - n, 0), 0, 0)),
            ],
            scratch_shapes=[
                pltpu.VMEM((tiles_row + 1, tile, cols), F32),
                pltpu.VMEM((tiles_row, cols, tile), BF16),
            ],
        ),
        out_shape=[
            jax.ShapeDtypeStruct((rows, cols), BF16),
            jax.ShapeDtypeStruct((n, rows, cols), BF16),
        ],
        compiler_params=local(),
        name="products",
    )(idx, where, gathered, gathered, tiles, sc, cotangent)

    chunk = rows // (2 * CUTS)
    grad_features, grad_weight = pl.pallas_call(
        functools.partial(scatter_kernel, n, nf, tile, (rows * n) ** (-0.5)),
        out_shape=[
            jax.ShapeDtypeStruct((quarter, width), BF16),
            jax.ShapeDtypeStruct((width, cols), F32),
        ],
        in_specs=[VMEM] * 4,
        out_specs=[VMEM] * 2,
        scratch_shapes=[
            pltpu.VMEM((2, n - 1, CUTS, chunk, cols), BF16),
            pltpu.VMEM((cols, rows), BF16),
            pltpu.VMEM((rows, cols), BF16),
            pltpu.VMEM((nf, quarter, cols), BF16),
            pltpu.VMEM((width, cols), BF16),
            pltpu.VMEM((n - 1, width // n, cols), BF16),
            pltpu.VMEM((width // n, cols), BF16),
            pltpu.VMEM((width, cols), BF16),
            dma((2, n - 1, CUTS)), dma((2, n - 1, CUTS)),
            dma((nf - 1,)), dma((nf - 1,)),
            dma((n - 1,)), dma((n - 1,)), dma((n - 1,)), dma((n - 1,)),
        ],
        compiler_params=pltpu.CompilerParams(
            collective_id=1, has_side_effects=True, vmem_limit_bytes=LIMIT
        ),
        name="scatter",
    )(terms, sct, fblock, weight)
    return (output, grad_features, grad_weight)


def solution(mesh):
    in_specs = (
        P(("blk", "feat"), None),
        P(),
        P("blk", None, None, None),
        P("blk", None),
        P("blk", None),
        P("blk", None),
        P("blk", "feat"),
    )
    out_specs = (P("blk", "feat"), P(("blk", "feat"), None), P(None, "feat"))
    return jax.shard_map(
        per_device, mesh=mesh, in_specs=in_specs, out_specs=out_specs, check_vma=False
    )
```

time: 346 us -> 115 us (0.33)
  waiting for transfers between devices: 209 us -> 0 us
  Pallas kernels: 0 us -> 105 us
  matrix products: 63.1 us -> 0 us
  local copies, waits for them, and re-layouts: 24.7 us -> 4.22 us
  blocking collectives: 18.8 us -> 0 us
  between operations: 13.9 us -> 0.66 us
  other arithmetic: 14.5 us -> 3.93 us
    pallas_call x0 -> x4, Pallas kernels: none -> 105 us  [the longest x1 42.5 us: per_device(): pl.pallas_call(functools.partial(scatter_kernel, n, nf, tile, (rows * n)...]
    reduce_scatter x2 -> x0, waiting for transfers between devices: 86.2 us -> none  [the longest x1 66.4 us: per_device(): lax.psum_scatter(lax.fori_loop(0, rows_dev * lax.axis_size('blk') // rows...]
    psum x1 -> x0, waiting for transfers between devices: 72.3 us -> none  [per_device(): summed_rows = lax.psum(partial_grad.astype(jnp.bfloat16), 'blk')]
    dot_general x53 -> x0, matrix products: 63.1 us -> none  [the longest x8 13.3 us: backward_part(): jnp.einsum('rs,sjf->rjf', placing, product, precision=lax.Precision.HIGHEST)]
    all_gather x1 -> x0, waiting for transfers between devices: 50 us -> none  [per_device(): shard_rows = lax.all_gather(scaled, 'blk', axis=0, tiled=True)]
    dynamic_slice x57 -> x0, local copies, waits for them, and re-layouts: 19.7 us -> none  [the longest x16 9.32 us: pair_slots(): lax.dynamic_slice_in_dim(counts, column, 1, 0)]
    all_to_all x2 -> x0, blocking collectives: 18.8 us -> none  [the longest x1 10.2 us: per_device(): lax.all_to_all(local_rows, 'feat', split_axis=1, concat_axis=0, tiled=True)]
    convert_element_type x19 -> x0, other arithmetic: 12.8 us -> none  [the longest x16 10.3 us: pair_slots(): (jnp.arange(capacity) < lax.dynamic_slice_in_dim(counts, column, 1, 0)).a...]
  transfers between devices with their start and end apart: 4 -> 0, of which waited for: 4 -> 0; matrix products, arithmetic and copies ran while one was open for 0% -> 0% of each run, Pallas kernels for 0% -> 0%
where the time goes in v1:
time: 115 us; the launch traced here: 114 us
  Pallas kernels  105 us (91%)
  local copies, waits for them, and re-layouts  4.22 us (4%)
  other arithmetic  3.93 us (3%)
    pallas_call x1, Pallas kernels, per_device(): pl.pallas_call(functools.partial(scatter_kernel, n, nf, tile, (rows * n)...  42.5 us
    pallas_call x1, Pallas kernels, per_device(): pl.pallas_call(functools.partial(gather_kernel, n, nf), out_shape=[jax.Sh...  39.5 us
    pallas_call x1, Pallas kernels, per_device(): pl.pallas_call(functools.partial(product_kernel, n, cap, tiles_row), grid...  16.1 us
    pallas_call x1, Pallas kernels, per_device(): pl.pallas_call(functools.partial(scaling_kernel, n, cap, tiles_row), grid...  7.35 us
    unnamed x2, local copies, waits for them, and re-layouts  3.34 us

profile of v1, /device:TPU:0, one launch (start us, length us, event | category | flops | bytes accessed | tf_op | source)
XLA Modules:
  0.0 114.3 jit_solution(11032039687875993886)
XLA Ops:
  0.6 0.7 broadcast_in_dim.13
  1.4 0.1 reshape.49
  1.4 0.1 reshape.48
  1.5 1.3 %compare_select_fusion.rows_ref = s32[160]{0:T(256)} fusion(s32[160]{0:T(256)} %bitcast.9, s32[160]{0:T(256)S(1)} %reshape.49), kind=kLoop, calls=%fused_computation.2 | loop fusion | flops 1280 | bytes 1920 | tf_op jit(solution)/shard_map/jit(_where)/select_n | solution.py:299
  2.8 0.7 broadcast_select_fusion.1
  3.5 0.7 broadcast_select_fusion
  4.2 1.3 %pad_add_fusion.idx = s32[4,160]{1,0:T(4,128)} fusion(s32[1,160]{1,0:T(1,128)S(1)} %broadcast_select_fusion, s32[1,160]{1,0:T(1,128)} %param.12, s32[1,160]{1,0:T(1,128)S(1)} %get-tuple-element.19, s32[1,160]{1,0:T(1,128)} %param.11), kind=kLoop, calls=%fused_computation | loop fusion | flops 1920 | bytes 5120 | tf_op jit(solution)/shard_map/stack | solution.py:298
  5.4 7.4 %scaling.1 = (f32[8,128,128]{2,1,0:T(8,128)}, f32[8,8,128]{2,1,0:T(8,128)}) custom-call(s32[160]{0:T(256)} %compare_select_fusion.rows_ref, bf16[160,128,128]{2,1,0:T(8,128)(2,1)} %bitcast.5), custom_call_target="tpu_custom_call" | custom-call | tf_op jit(solution)/shard_map/scaling/pallas_call | solution.py:307
  12.8 39.5 %gather.1 = (bf16[8,1024,128]{2,1,0:T(8,128)(2,1)}, bf16[1024,512]{1,0:T(8,128)(2,1)}) custom-call(bf16[256,512]{1,0:T(8,128)(2,1)} %feat_ref.1, bf16[512,512]{1,0:T(8,128)(2,1)} %w_ref.3, f32[1024,128]{1,0:T(8,128)} %bitcast.7), custom_call_target="tpu_custom_call" | custom-call | tf_op jit(solution)/shard_map/gather/pallas_call | solution.py:328
  52.3 16.1 %products.1 = (bf16[1024,128]{1,0:T(8,128)(2,1)}, bf16[8,1024,128]{2,1,0:T(8,128)(2,1)}) custom-call(s32[4,160]{1,0:T(4,128)} %pad_add_fusion.idx, s32[1]{0:T(128)} %bitcast.1.where, bf16[8,1024,128]{2,1,0:T(8,128)(2,1)} %get-tuple-element.12.s_ref.own_ref, bf16[8,1024,128]{2,1,0:T(8,128)(2,1)} %get-tuple-element.12.s_ref.own_ref, ...), custom_call_target="tpu_custom_call" | custom-call | tf_op jit(solution)/shard_map/products/pallas_call | solution.py:347
  68.4 42.5 %scatter.1 = (bf16[256,512]{1,0:T(8,128)(2,1)}, f32[512,128]{1,0:T(8,128)}) custom-call(bf16[8,1024,128]{2,1,0:T(8,128)(2,1)} %get-tuple-element.14.terms_ref, f32[8,8,128]{2,1,0:T(8,128)} %get-tuple-element.15.sct_ref, bf16[1024,512]{1,0:T(8,128)(2,1)} %get-tuple-element.16.fb_ref, bf16[512,512]{1,0:T(8,128)(2,1)} %w_ref.3), custom_call_target="tpu_custom_call" | custom-call | tf_op jit(solution)/shard_map/scatter/pallas_call | solution.py:377
  110.9 1.7 %copy.12 = bf16[256,512]{1,0:T(8,128)(2,1)} copy(bf16[256,512]{1,0:T(8,128)(2,1)} %get-tuple-element.25) | data formatting | bytes 524288
  112.6 1.7 %copy.13 = f32[512,128]{1,0:T(8,128)} copy(f32[512,128]{1,0:T(8,128)} %get-tuple-element.26) | data formatting | bytes 524288

commit v2 on v1

v2 whole, which is shorter than its diff:
```python
import functools

import jax
import jax.numpy as jnp
from jax import lax
from jax.experimental import pallas as pl
from jax.experimental.pallas import tpu as pltpu
from jax.sharding import PartitionSpec as P

MESH = pl.DeviceIdType.MESH
VMEM = pl.BlockSpec(memory_space=pltpu.VMEM)
F32, BF16 = jnp.float32, jnp.bfloat16
LIMIT = 56 * 1024 * 1024
CUTS = 2
GELU_C = 0.7978845608028654
GELU_A = 0.044715


def ring_of(n):
    me = lax.axis_index("blk")
    half = n // 2
    pos = jnp.where(me % 2 == 0, me // 2, n - 1 - me // 2)

    def blk_of(p):
        p = (p + 2 * n) % n
        return jnp.where(p < half, 2 * p, 2 * (n - 1 - p) + 1)

    return me, pos, blk_of


def greet(peers):
    barrier = pltpu.get_barrier_semaphore()
    for peer in peers:
        pl.semaphore_signal(barrier, inc=1, device_id=peer, device_id_type=MESH)
    pl.semaphore_wait(barrier, len(peers))


def remote(src, dst, send, recv, peer):
    return pltpu.make_async_remote_copy(
        src_ref=src, dst_ref=dst, send_sem=send, recv_sem=recv, device_id=peer, device_id_type=MESH
    )


def dense_kernel(n, cap, tiles_row, cnt_ref, row_ref, col_ref, tiles_ref, dense_ref, sc_ref, sct_ref, acc):
    c = pl.program_id(0)
    tile = tiles_ref.shape[1]
    across = tiles_row // 2

    @pl.when(c == 0)
    def _():
        acc[...] = jnp.zeros_like(acc)

    dense_ref[...] = jnp.zeros_like(dense_ref)
    count = cnt_ref[0, c]
    for k in range(cap):

        @pl.when(k < count)
        def _():
            row, col = row_ref[0, c * cap + k], col_ref[0, c * cap + k]
            value = tiles_ref[k]
            acc[row] += value.astype(F32)
            rows_at = pl.ds(pl.multiple_of(row * tile, tile), tile)
            cols_at = pl.ds(pl.multiple_of(col % across * tile, tile), tile)
            dense_ref[0, col // across, rows_at, cols_at] += value

    @pl.when(c == n - 1)
    def _():
        for t in range(tiles_row):
            degree = 1.0 + jnp.sum(acc[t], axis=1, keepdims=True)
            wide = jnp.broadcast_to(lax.rsqrt(degree), acc.shape[1:])
            sc_ref[t * tile:(t + 1) * tile, :] = wide
            sct_ref[:, t * tile:(t + 1) * tile] = wide.T[0:8]


def layer_kernel(
    n, nf, tile, feat_ref, w_ref, sc_ref, sct_ref, cot_ref, dense_ref, out_ref, gf_ref, wfin,
    all_ref, fb_ref, buf, abuf, acc, gt, stage, tbuf, land, hgt, hg, hg4, wbuf, wland, wsum,
    asem, s1, r1, s2, r2, s3, r3, s4, r4, s5, r5, s6, r6, s7, r7,
):
    me, pos, blk_of = ring_of(n)
    mf = lax.axis_index("feat")
    quarter = feat_ref.shape[0]
    rows, cols = all_ref.shape[1:]
    half = rows // 2
    right, left = (blk_of(pos + 1), mf), (blk_of(pos - 1), mf)
    fpeers = [(me, (mf + d) % nf) for d in range(1, nf)]
    bpeers = [((me + d) % n, mf) for d in range(1, n)]
    greet(fpeers + bpeers)

    def block_of(d, u):
        return blk_of(pos - u) if d == 0 else blk_of(pos + u)

    def fetch(d, v):
        u = jnp.where(v < n, v, v - n + 1)
        slot = v % 2
        return pltpu.make_async_copy(dense_ref.at[block_of(d, u), d], abuf.at[slot, d], asem.at[slot, d])

    def begin(v):
        for d in range(2):
            fetch(d, v).start()

    begin(0)
    mine = pl.ds(pl.multiple_of(mf * quarter, quarter), quarter)
    scale = sc_ref[mine, :]

    def rows_for(f):
        w = w_ref[:, pl.ds(pl.multiple_of(f * cols, cols), cols)]
        h = jnp.dot(feat_ref[...], w, preferred_element_type=F32)
        return (scale * h).astype(BF16)

    first = []
    for d in (2, 3, 1):
        peer = fpeers[d - 1]
        buf[d - 1] = rows_for(peer[1])
        copy = remote(buf.at[d - 1], all_ref.at[me, mine], s1.at[d - 1], r1.at[d - 1], peer)
        copy.start()
        first.append(copy)
    all_ref[me, mine, :] = rows_for(mf)
    fb_ref[mine, :] = feat_ref[...]
    for copy in first:
        copy.wait_recv()

    chunk = half // CUTS

    def gather_copy(d, s, q):
        part = all_ref.at[block_of(d, s), pl.ds(d * half + q * chunk, chunk)]
        return remote(part, part, s2.at[d, s, q], r2.at[d, s, q], right if d == 0 else left)

    for q in range(CUTS):
        for d in range(2):
            gather_copy(d, 0, q).start()
    later = []
    for d in range(1, nf):
        copy = remote(feat_ref, fb_ref.at[mine], s3.at[d - 1], r3.at[d - 1], fpeers[d - 1])
        copy.start()
        later.append(copy)

    def fold(v):
        begin(v + 1)
        for d in range(2):
            fetch(d, v).wait()
            acc[...] += jnp.dot(
                abuf[v % 2, d],
                all_ref[block_of(d, v), d * half:(d + 1) * half, :],
                preferred_element_type=F32,
            )

    acc[...] = all_ref[me].astype(F32)
    fold(0)

    def gather_step(s, carry):
        for q in range(CUTS):
            for d in range(2):
                gather_copy(d, s - 1, q).wait_recv()
                gather_copy(d, s, q).start()
        fold(s)
        return carry

    lax.fori_loop(1, n - 1, gather_step, 0)
    for q in range(CUTS):
        for d in range(2):
            gather_copy(d, n - 2, q).wait_recv()
    fold(n - 1)

    for t in range(rows // tile):
        part = slice(t * tile, (t + 1) * tile)
        scale = sc_ref[part, :]
        v = scale * acc[part, :]
        square = v * v
        th = jnp.tanh(GELU_C * (v + GELU_A * (square * v)))
        level = 0.5 * (1.0 + th)
        out_ref[part, :] = (v * level).astype(BF16)
        slope = level + 0.5 * v * (1.0 - th * th) * (GELU_C * (1.0 + 3.0 * GELU_A * square))
        gt[:, part] = (scale * (slope * cot_ref[part, :].astype(F32))).T.astype(BF16)

    strip = cols // CUTS

    def scatter_copy(src, d, s, q):
        return remote(src, land.at[d, s, q], s4.at[d, s, q], r4.at[d, s, q], right if d == 0 else left)

    def term(v, d):
        fetch(d, v).wait()
        return jnp.dot(gt[...], abuf[v % 2, d], preferred_element_type=F32)

    begin(n + 1)
    for d in range(2):
        value = term(n, d).astype(BF16)
        for q in range(CUTS):
            stage[d, q] = value[q * strip:(q + 1) * strip]
            scatter_copy(stage.at[d, q], d, 0, q).start()

    def scatter_step(s, carry):
        begin(n + s + 1)
        for d in range(2):
            tbuf[d] = term(n + s, d)
        for q in range(CUTS):
            for d in range(2):
                slot = land.at[d, s - 1, q]
                scatter_copy(slot, d, s - 1, q).wait_recv()
                slot[...] = (slot[...].astype(F32) + tbuf[d, q * strip:(q + 1) * strip, :]).astype(BF16)
                scatter_copy(slot, d, s, q).start()
        return carry

    lax.fori_loop(1, n - 1, scatter_step, 0)
    for d in range(2):
        tbuf[d] = term(2 * n - 1, d) + gt[:, d * half:(d + 1) * half].astype(F32)
    for q in range(CUTS):
        for d in range(2):
            slot = land.at[d, n - 2, q]
            scatter_copy(slot, d, n - 2, q).wait_recv()
            part = slice(d * half, (d + 1) * half)
            total = slot[...].astype(F32) + tbuf[d, q * strip:(q + 1) * strip, :]
            tbuf[d, q * strip:(q + 1) * strip, :] = total * sct_ref[0:1, part]
    for t in range(rows // tile):
        d, at = t * tile // half, t * tile % half
        total = tbuf[d, :, at:at + tile]
        hgt[:, t * tile:(t + 1) * tile] = total.astype(BF16)
        hg[t * tile:(t + 1) * tile, :] = total.T.astype(BF16)

    sent = []
    for d in (2, 3, 1):
        peer = fpeers[d - 1]
        src = hg.at[pl.ds(pl.multiple_of(peer[1] * quarter, quarter), quarter)]
        copy = remote(src, hg4.at[mf], s5.at[d - 1], r5.at[d - 1], peer)
        copy.start()
        sent.append(copy)
    hg4[mf] = hg[mine, :]
    for copy in later:
        copy.wait_recv()
    wgt = jnp.dot(hgt[...], fb_ref[...], preferred_element_type=F32)
    wbuf[...] = wgt.T.astype(BF16)
    piece = wsum.shape[0]

    def piece_of(b):
        return pl.ds(pl.multiple_of(b * piece, piece), piece)

    pieces = []
    for d in range(1, n):
        peer = bpeers[d - 1]
        copy = remote(wbuf.at[piece_of(peer[0])], wland.at[d - 1], s6.at[d - 1], r6.at[d - 1], peer)
        copy.start()
        pieces.append(copy)
    summed = wbuf[piece_of(me), :].astype(F32)
    for d in range(1, n):
        pieces[d - 1].wait_recv()
        summed = summed + wland[d - 1].astype(F32)
    wsum[...] = summed.astype(BF16)
    finals = []
    for d in range(1, n):
        copy = remote(wsum, wfin.at[piece_of(me)], s7.at[d - 1], r7.at[d - 1], bpeers[d - 1])
        copy.start()
        finals.append(copy)
    wfin[piece_of(me), :] = wsum[...]
    for copy in sent:
        copy.wait_recv()
    total = None
    for f in range(nf):
        part = lax.dot_general(
            hg4[f], w_ref[:, f * cols:(f + 1) * cols], (((1,), (1,)), ((), ())),
            preferred_element_type=F32,
        )
        total = part if total is None else total + part
    gf_ref[...] = total.astype(BF16)

    def drain(s, carry):
        for q in range(CUTS):
            for d in range(2):
                gather_copy(d, s, q).wait_send()
                scatter_copy(land.at[d, s, q], d, s, q).wait_send()
        return carry

    lax.fori_loop(0, n - 1, drain, 0)
    for copy in first + later + sent + pieces:
        copy.wait_send()
    for copy in finals:
        copy.wait_recv()
    for copy in finals:
        copy.wait_send()


def finish_kernel(factor, out_in, gf_in, w_in, out_ref, gf_ref, gw_ref):
    out_ref[...] = out_in[...]
    gf_ref[...] = gf_in[...]
    gw_ref[...] = w_in[...].astype(F32) * factor


def per_device(features, weight, tile_vals, pair_counts, slot_row, slot_col, cotangent):
    n = lax.axis_size("blk")
    nf = lax.axis_size("feat")
    tiles = tile_vals[0]
    slots, tile, _ = tiles.shape
    cap = slots // n
    rows, cols = cotangent.shape
    quarter, width = features.shape
    tiles_row = rows // tile
    half = rows // 2
    dma = pltpu.SemaphoreType.DMA
    shape = jax.ShapeDtypeStruct

    dense, sc, sct = pl.pallas_call(
        functools.partial(dense_kernel, n, cap, tiles_row),
        grid_spec=pltpu.PrefetchScalarGridSpec(
            num_scalar_prefetch=3,
            grid=(n,),
            in_specs=[pl.BlockSpec((cap, tile, tile), lambda i, *_: (i, 0, 0))],
            out_specs=[
                pl.BlockSpec((1, 2, rows, half), lambda i, *_: (i, 0, 0, 0)),
                pl.BlockSpec((rows, tile), lambda i, *_: (0, 0)),
                pl.BlockSpec((8, rows), lambda i, *_: (0, 0)),
            ],
            scratch_shapes=[pltpu.VMEM((tiles_row, tile, tile), F32)],
        ),
        out_shape=[shape((n, 2, rows, half), BF16), shape((rows, tile), F32), shape((8, rows), F32)],
        compiler_params=pltpu.CompilerParams(
            dimension_semantics=("arbitrary",), vmem_limit_bytes=LIMIT
        ),
        name="dense",
    )(pair_counts, slot_row, slot_col, tiles)

    ring = dma((2, n - 1, CUTS))
    peers, others = dma((nf - 1,)), dma((n - 1,))
    vmem = pltpu.VMEM
    output, grad_features, summed = pl.pallas_call(
        functools.partial(layer_kernel, n, nf, tile),
        out_shape=[shape((rows, cols), BF16), shape((quarter, width), BF16), shape((width, cols), BF16)],
        in_specs=[VMEM] * 5 + [pl.BlockSpec(memory_space=pl.ANY)],
        out_specs=[VMEM] * 3,
        scratch_shapes=[
            vmem((n, rows, cols), BF16),
            vmem((rows, width), BF16),
            vmem((nf - 1, quarter, cols), BF16),
            vmem((2, 2, rows, half), BF16),
            vmem((rows, cols), F32),
            vmem((cols, rows), BF16),
            vmem((2, CUTS, cols // CUTS, half), BF16),
            vmem((2, cols, half), F32),
            vmem((2, n - 1, CUTS, cols // CUTS, half), BF16),
            vmem((cols, rows), BF16),
            vmem((rows, cols), BF16),
            vmem((nf, quarter, cols), BF16),
            vmem((width, cols), BF16),
            vmem((n - 1, width // n, cols), BF16),
            vmem((width // n, cols), BF16),
            dma((2, 2)),
            peers, peers, ring, ring, peers, peers, ring, ring, peers, peers,
            others, others, others, others,
        ],
        compiler_params=pltpu.CompilerParams(
            collective_id=0, has_side_effects=True, vmem_limit_bytes=LIMIT
        ),
        name="layer",
    )(features, weight, sc, sct, cotangent, dense)

    return tuple(
        pl.pallas_call(
            functools.partial(finish_kernel, (rows * n) ** (-0.5)),
            out_shape=[shape((rows, cols), BF16), shape((quarter, width), BF16), shape((width, cols), F32)],
            in_specs=[VMEM] * 3,
            out_specs=[VMEM] * 3,
            name="finish",
        )(output, grad_features, summed)
    )


def solution(mesh):
    in_specs = (
        P(("blk", "feat"), None),
        P(),
        P("blk", None, None, None),
        P("blk", None),
        P("blk", None),
        P("blk", None),
        P("blk", "feat"),
    )
    out_specs = (P("blk", "feat"), P(("blk", "feat"), None), P(None, "feat"))
    return jax.shard_map(
        per_device, mesh=mesh, in_specs=in_specs, out_specs=out_specs, check_vma=False
    )
```

time: 115 us -> 94.1 us (0.82)
  Pallas kernels: 105 us -> 93.1 us
  local copies, waits for them, and re-layouts: 4.22 us -> 0 us
  other arithmetic: 3.93 us -> 0 us
    pallas_call x4 -> x3, Pallas kernels: 105 us -> 93.1 us  [the longest x1 79.7 us: per_device(): pl.pallas_call(functools.partial(layer_kernel, n, nf, tile), out_shape=[s...]
    unnamed x2 -> x0, local copies, waits for them, and re-layouts: 3.34 us -> none
    select_n x3 -> x0, other arithmetic: 2.63 us -> none  [the longest x2 1.95 us: per_device(): jnp.where(filled, row_ids, tiles_row)]
    another operation x1 -> x0, other arithmetic: 1.3 us -> none  [per_device(): jnp.stack([row_ids, jnp.where(filled, row_ids, tiles_row), col_ids, jnp.w...]
where the time goes in v2:
time: 94.1 us; the launch traced here: 93.7 us
  Pallas kernels  93.1 us (99%)
    pallas_call x1, Pallas kernels, per_device(): pl.pallas_call(functools.partial(layer_kernel, n, nf, tile), out_shape=[s...  79.7 us
    pallas_call x1, Pallas kernels, per_device(): pl.pallas_call(functools.partial(dense_kernel, n, cap, tiles_row), grid_s...  11.4 us
    pallas_call x1, Pallas kernels, per_device(): pl.pallas_call(functools.partial(finish_kernel, (rows * n) ** (-0.5)), ou...  1.96 us

profile of v2, /device:TPU:0, one launch (start us, length us, event | category | flops | bytes accessed | tf_op | source)
XLA Modules:
  0.0 93.7 jit_solution(2974404426719188197)
XLA Ops:
  0.6 11.4 %dense.1 = (bf16[8,2,1024,512]{3,2,1,0:T(8,128)(2,1)}, f32[1024,128]{1,0:T(8,128)}, f32[8,1024]{1,0:T(8,128)}) custom-call(s32[1,8]{1,0:T(1,128)} %cnt_ref.1, s32[1,160]{1,0:T(1,128)} %row_ref.1, s32[1,160]{1,0:T(1,128)} %col_ref.1, bf16[160,128,128]{2,1,0:T(8,128)(2,1)} %bitcast.1), custom_call_target="tpu_custom_call" | custom-call | tf_op jit(solution)/shard_map/dense/pallas_call | solution.py:300
  12.1 79.7 %layer.1 = (bf16[1024,128]{1,0:T(8,128)(2,1)}, bf16[256,512]{1,0:T(8,128)(2,1)}, bf16[512,128]{1,0:T(8,128)(2,1)}) custom-call(bf16[256,512]{1,0:T(8,128)(2,1)} %feat_ref.1, bf16[512,512]{1,0:T(8,128)(2,1)} %w_ref.1, f32[1024,128]{1,0:T(8,128)} %get-tuple-element.9.sc_ref, f32[8,1024]{1,0:T(8,128)} %get-tuple-element.10.sct_ref, bf16[1024,128]{1,0:T(8,128)(2,1)} %cot_ref.1, ...), custom_call_target="tpu_custom_call" | custom-call | tf_op jit(solution)/shard_map/layer/pallas_call | solution.py:323
  91.8 2.0 %finish.1 = (bf16[1024,128]{1,0:T(8,128)(2,1)}, bf16[256,512]{1,0:T(8,128)(2,1)}, f32[512,128]{1,0:T(8,128)}) custom-call(bf16[1024,128]{1,0:T(8,128)(2,1)} %get-tuple-element.12.out_in, bf16[256,512]{1,0:T(8,128)(2,1)} %get-tuple-element.13.gf_in, bf16[512,128]{1,0:T(8,128)(2,1)} %get-tuple-element.14.w_in), custom_call_target="tpu_custom_call" | custom-call | tf_op jit(solution)/shard_map/finish/pallas_call | solution.py:355

commit v3 on v2

--- a/solution.py
+++ b/solution.py
@@ -11,7 +11,7 @@
 VMEM = pl.BlockSpec(memory_space=pltpu.VMEM)
 F32, BF16 = jnp.float32, jnp.bfloat16
 LIMIT = 56 * 1024 * 1024
-CUTS = 2
+CUTS = 4
 GELU_C = 0.7978845608028654
 GELU_A = 0.044715
 

time: 94.1 us -> 89.6 us (0.952)
  Pallas kernels: 93.1 us -> 88.5 us
    pallas_call x1, Pallas kernels: 79.7 us -> 75 us  [per_device(): pl.pallas_call(functools.partial(layer_kernel, n, nf, tile), out_shape=[s...]
where the time goes in v3:
time: 89.6 us; the launch traced here: 89.2 us
  Pallas kernels  88.5 us (99%)
    pallas_call x1, Pallas kernels, per_device(): pl.pallas_call(functools.partial(layer_kernel, n, nf, tile), out_shape=[s...  75 us
    pallas_call x1, Pallas kernels, per_device(): pl.pallas_call(functools.partial(dense_kernel, n, cap, tiles_row), grid_s...  11.6 us
    pallas_call x1, Pallas kernels, per_device(): pl.pallas_call(functools.partial(finish_kernel, (rows * n) ** (-0.5)), ou...  1.96 us

profile of v3, /device:TPU:0, one launch (start us, length us, event | category | flops | bytes accessed | tf_op | source)
XLA Modules:
  0.0 89.2 jit_solution(10586447178205732877)
XLA Ops:
  0.6 11.6 %dense.1 = (bf16[8,2,1024,512]{3,2,1,0:T(8,128)(2,1)}, f32[1024,128]{1,0:T(8,128)}, f32[8,1024]{1,0:T(8,128)}) custom-call(s32[1,8]{1,0:T(1,128)} %cnt_ref.1, s32[1,160]{1,0:T(1,128)} %row_ref.1, s32[1,160]{1,0:T(1,128)} %col_ref.1, bf16[160,128,128]{2,1,0:T(8,128)(2,1)} %bitcast.1), custom_call_target="tpu_custom_call" | custom-call | tf_op jit(solution)/shard_map/dense/pallas_call | solution.py:300
  12.2 75.0 %layer.1 = (bf16[1024,128]{1,0:T(8,128)(2,1)}, bf16[256,512]{1,0:T(8,128)(2,1)}, bf16[512,128]{1,0:T(8,128)(2,1)}) custom-call(bf16[256,512]{1,0:T(8,128)(2,1)} %feat_ref.1, bf16[512,512]{1,0:T(8,128)(2,1)} %w_ref.1, f32[1024,128]{1,0:T(8,128)} %get-tuple-element.9.sc_ref, f32[8,1024]{1,0:T(8,128)} %get-tuple-element.10.sct_ref, bf16[1024,128]{1,0:T(8,128)(2,1)} %cot_ref.1, ...), custom_call_target="tpu_custom_call" | custom-call | tf_op jit(solution)/shard_map/layer/pallas_call | solution.py:323
  87.2 2.0 %finish.1 = (bf16[1024,128]{1,0:T(8,128)(2,1)}, bf16[256,512]{1,0:T(8,128)(2,1)}, f32[512,128]{1,0:T(8,128)}) custom-call(bf16[1024,128]{1,0:T(8,128)(2,1)} %get-tuple-element.12.out_in, bf16[256,512]{1,0:T(8,128)(2,1)} %get-tuple-element.13.gf_in, bf16[512,128]{1,0:T(8,128)(2,1)} %get-tuple-element.14.w_in), custom_call_target="tpu_custom_call" | custom-call | tf_op jit(solution)/shard_map/finish/pallas_call | solution.py:355

commit v4 on v3

--- a/solution.py
+++ b/solution.py
@@ -11,7 +11,7 @@
 VMEM = pl.BlockSpec(memory_space=pltpu.VMEM)
 F32, BF16 = jnp.float32, jnp.bfloat16
 LIMIT = 56 * 1024 * 1024
-CUTS = 4
+CUTS = 8
 GELU_C = 0.7978845608028654
 GELU_A = 0.044715
 

time: 89.6 us -> 89.8 us (level)
  no operation moved by 1% of the time
where the time goes in v4:
time: 89.8 us
  Pallas kernels  89.1 us (99%)
    pallas_call x1, Pallas kernels, per_device(): pl.pallas_call(functools.partial(layer_kernel, n, nf, tile), out_shape=[s...  75.7 us
    pallas_call x1, Pallas kernels, per_device(): pl.pallas_call(functools.partial(dense_kernel, n, cap, tiles_row), grid_s...  11.5 us
    pallas_call x1, Pallas kernels, per_device(): pl.pallas_call(functools.partial(finish_kernel, (rows * n) ** (-0.5)), ou...  1.96 us

profile of v4, /device:TPU:0, one launch (start us, length us, event | category | flops | bytes accessed | tf_op | source)
XLA Modules:
  0.0 89.8 jit_solution(10057664143284150107)
XLA Ops:
  0.6 11.5 %dense.1 = (bf16[8,2,1024,512]{3,2,1,0:T(8,128)(2,1)}, f32[1024,128]{1,0:T(8,128)}, f32[8,1024]{1,0:T(8,128)}) custom-call(s32[1,8]{1,0:T(1,128)} %cnt_ref.1, s32[1,160]{1,0:T(1,128)} %row_ref.1, s32[1,160]{1,0:T(1,128)} %col_ref.1, bf16[160,128,128]{2,1,0:T(8,128)(2,1)} %bitcast.1), custom_call_target="tpu_custom_call" | custom-call | tf_op jit(solution)/shard_map/dense/pallas_call | solution.py:300
  12.1 75.7 %layer.1 = (bf16[1024,128]{1,0:T(8,128)(2,1)}, bf16[256,512]{1,0:T(8,128)(2,1)}, bf16[512,128]{1,0:T(8,128)(2,1)}) custom-call(bf16[256,512]{1,0:T(8,128)(2,1)} %feat_ref.1, bf16[512,512]{1,0:T(8,128)(2,1)} %w_ref.1, f32[1024,128]{1,0:T(8,128)} %get-tuple-element.9.sc_ref, f32[8,1024]{1,0:T(8,128)} %get-tuple-element.10.sct_ref, bf16[1024,128]{1,0:T(8,128)(2,1)} %cot_ref.1, ...), custom_call_target="tpu_custom_call" | custom-call | tf_op jit(solution)/shard_map/layer/pallas_call | solution.py:323
  87.8 2.0 %finish.1 = (bf16[1024,128]{1,0:T(8,128)(2,1)}, bf16[256,512]{1,0:T(8,128)(2,1)}, f32[512,128]{1,0:T(8,128)}) custom-call(bf16[1024,128]{1,0:T(8,128)(2,1)} %get-tuple-element.12.out_in, bf16[256,512]{1,0:T(8,128)(2,1)} %get-tuple-element.13.gf_in, bf16[512,128]{1,0:T(8,128)(2,1)} %get-tuple-element.14.w_in), custom_call_target="tpu_custom_call" | custom-call | tf_op jit(solution)/shard_map/finish/pallas_call | solution.py:355

commit v5 on v3

--- a/solution.py
+++ b/solution.py
@@ -117,18 +117,23 @@
         first.append(copy)
     all_ref[me, mine, :] = rows_for(mf)
     fb_ref[mine, :] = feat_ref[...]
-    for copy in first:
-        copy.wait_recv()
-
     chunk = half // CUTS
 
     def gather_copy(d, s, q):
         part = all_ref.at[block_of(d, s), pl.ds(d * half + q * chunk, chunk)]
         return remote(part, part, s2.at[d, s, q], r2.at[d, s, q], right if d == 0 else left)
 
-    for q in range(CUTS):
-        for d in range(2):
-            gather_copy(d, 0, q).start()
+    def start_quarter(f):
+        for j in range(quarter // chunk):
+            place = f * (quarter // chunk) + j
+            d, q = place // CUTS, place % CUTS
+            part = all_ref.at[me, pl.ds(pl.multiple_of(place * chunk, chunk), chunk)]
+            remote(part, part, s2.at[d, 0, q], r2.at[d, 0, q], (blk_of(pos + 1 - 2 * d), mf)).start()
+
+    start_quarter(mf)
+    for copy, d in zip(first, (2, 3, 1)):
+        copy.wait_recv()
+        start_quarter((mf + nf - d) % nf)
     later = []
     for d in range(1, nf):
         copy = remote(feat_ref, fb_ref.at[mine], s3.at[d - 1], r3.at[d - 1], fpeers[d - 1])

time: 89.6 us -> 90.1 us (level)
  no operation moved by 1% of the time
where the time goes in v5:
time: 90.1 us; the launch traced here: 89.4 us
  Pallas kernels  88.7 us (98%)
    pallas_call x1, Pallas kernels, per_device(): pl.pallas_call(functools.partial(layer_kernel, n, nf, tile), out_shape=[s...  75.1 us
    pallas_call x1, Pallas kernels, per_device(): pl.pallas_call(functools.partial(dense_kernel, n, cap, tiles_row), grid_s...  11.7 us
    pallas_call x1, Pallas kernels, per_device(): pl.pallas_call(functools.partial(finish_kernel, (rows * n) ** (-0.5)), ou...  1.96 us

profile of v5, /device:TPU:0, one launch (start us, length us, event | category | flops | bytes accessed | tf_op | source)
XLA Modules:
  0.0 89.4 jit_solution(2392861151603186342)
XLA Ops:
  0.6 11.7 %dense.1 = (bf16[8,2,1024,512]{3,2,1,0:T(8,128)(2,1)}, f32[1024,128]{1,0:T(8,128)}, f32[8,1024]{1,0:T(8,128)}) custom-call(s32[1,8]{1,0:T(1,128)} %cnt_ref.1, s32[1,160]{1,0:T(1,128)} %row_ref.1, s32[1,160]{1,0:T(1,128)} %col_ref.1, bf16[160,128,128]{2,1,0:T(8,128)(2,1)} %bitcast.1), custom_call_target="tpu_custom_call" | custom-call | tf_op jit(solution)/shard_map/dense/pallas_call | solution.py:305
  12.3 75.1 %layer.1 = (bf16[1024,128]{1,0:T(8,128)(2,1)}, bf16[256,512]{1,0:T(8,128)(2,1)}, bf16[512,128]{1,0:T(8,128)(2,1)}) custom-call(bf16[256,512]{1,0:T(8,128)(2,1)} %feat_ref.1, bf16[512,512]{1,0:T(8,128)(2,1)} %w_ref.1, f32[1024,128]{1,0:T(8,128)} %get-tuple-element.9.sc_ref, f32[8,1024]{1,0:T(8,128)} %get-tuple-element.10.sct_ref, bf16[1024,128]{1,0:T(8,128)(2,1)} %cot_ref.1, ...), custom_call_target="tpu_custom_call" | custom-call | tf_op jit(solution)/shard_map/layer/pallas_call | solution.py:328
  87.4 2.0 %finish.1 = (bf16[1024,128]{1,0:T(8,128)(2,1)}, bf16[256,512]{1,0:T(8,128)(2,1)}, f32[512,128]{1,0:T(8,128)}) custom-call(bf16[1024,128]{1,0:T(8,128)(2,1)} %get-tuple-element.12.out_in, bf16[256,512]{1,0:T(8,128)(2,1)} %get-tuple-element.13.gf_in, bf16[512,128]{1,0:T(8,128)(2,1)} %get-tuple-element.14.w_in), custom_call_target="tpu_custom_call" | custom-call | tf_op jit(solution)/shard_map/finish/pallas_call | solution.py:360

commit v6 on v3

--- a/solution.py
+++ b/solution.py
@@ -32,7 +32,7 @@
     barrier = pltpu.get_barrier_semaphore()
     for peer in peers:
         pl.semaphore_signal(barrier, inc=1, device_id=peer, device_id_type=MESH)
-    pl.semaphore_wait(barrier, len(peers))
+    return lambda: pl.semaphore_wait(barrier, len(peers))
 
 
 def remote(src, dst, send, recv, peer):
@@ -85,7 +85,7 @@
     right, left = (blk_of(pos + 1), mf), (blk_of(pos - 1), mf)
     fpeers = [(me, (mf + d) % nf) for d in range(1, nf)]
     bpeers = [((me + d) % n, mf) for d in range(1, n)]
-    greet(fpeers + bpeers)
+    all_here = greet(fpeers + bpeers)
 
     def block_of(d, u):
         return blk_of(pos - u) if d == 0 else blk_of(pos + u)
@@ -108,15 +108,17 @@
         h = jnp.dot(feat_ref[...], w, preferred_element_type=F32)
         return (scale * h).astype(BF16)
 
+    for d in (2, 3, 1):
+        buf[d - 1] = rows_for(fpeers[d - 1][1])
+    all_ref[me, mine, :] = rows_for(mf)
+    fb_ref[mine, :] = feat_ref[...]
+    all_here()
     first = []
     for d in (2, 3, 1):
         peer = fpeers[d - 1]
-        buf[d - 1] = rows_for(peer[1])
         copy = remote(buf.at[d - 1], all_ref.at[me, mine], s1.at[d - 1], r1.at[d - 1], peer)
         copy.start()
         first.append(copy)
-    all_ref[me, mine, :] = rows_for(mf)
-    fb_ref[mine, :] = feat_ref[...]
     for copy in first:
         copy.wait_recv()
 

time: 89.6 us -> 89.2 us (level)
    pallas_call x1, Pallas kernels: 75 us -> 74.1 us  [per_device(): pl.pallas_call(functools.partial(layer_kernel, n, nf, tile), out_shape=[s...]
where the time goes in v6:
time: 89.2 us; the launch traced here: 88.6 us
  Pallas kernels  88 us (99%)
    pallas_call x1, Pallas kernels, per_device(): pl.pallas_call(functools.partial(layer_kernel, n, nf, tile), out_shape=[s...  74.1 us
    pallas_call x1, Pallas kernels, per_device(): pl.pallas_call(functools.partial(dense_kernel, n, cap, tiles_row), grid_s...  12 us
    pallas_call x1, Pallas kernels, per_device(): pl.pallas_call(functools.partial(finish_kernel, (rows * n) ** (-0.5)), ou...  1.96 us

profile of v6, /device:TPU:0, one launch (start us, length us, event | category | flops | bytes accessed | tf_op | source)
XLA Modules:
  0.0 88.6 jit_solution(6310359290311508862)
XLA Ops:
  0.6 12.0 %dense.1 = (bf16[8,2,1024,512]{3,2,1,0:T(8,128)(2,1)}, f32[1024,128]{1,0:T(8,128)}, f32[8,1024]{1,0:T(8,128)}) custom-call(s32[1,8]{1,0:T(1,128)} %cnt_ref.1, s32[1,160]{1,0:T(1,128)} %row_ref.1, s32[1,160]{1,0:T(1,128)} %col_ref.1, bf16[160,128,128]{2,1,0:T(8,128)(2,1)} %bitcast.1), custom_call_target="tpu_custom_call" | custom-call | tf_op jit(solution)/shard_map/dense/pallas_call | solution.py:302
  12.6 74.1 %layer.1 = (bf16[1024,128]{1,0:T(8,128)(2,1)}, bf16[256,512]{1,0:T(8,128)(2,1)}, bf16[512,128]{1,0:T(8,128)(2,1)}) custom-call(bf16[256,512]{1,0:T(8,128)(2,1)} %feat_ref.1, bf16[512,512]{1,0:T(8,128)(2,1)} %w_ref.1, f32[1024,128]{1,0:T(8,128)} %get-tuple-element.9.sc_ref, f32[8,1024]{1,0:T(8,128)} %get-tuple-element.10.sct_ref, bf16[1024,128]{1,0:T(8,128)(2,1)} %cot_ref.1, ...), custom_call_target="tpu_custom_call" | custom-call | tf_op jit(solution)/shard_map/layer/pallas_call | solution.py:325
  86.7 2.0 %finish.1 = (bf16[1024,128]{1,0:T(8,128)(2,1)}, bf16[256,512]{1,0:T(8,128)(2,1)}, f32[512,128]{1,0:T(8,128)}) custom-call(bf16[1024,128]{1,0:T(8,128)(2,1)} %get-tuple-element.12.out_in, bf16[256,512]{1,0:T(8,128)(2,1)} %get-tuple-element.13.gf_in, bf16[512,128]{1,0:T(8,128)(2,1)} %get-tuple-element.14.w_in), custom_call_target="tpu_custom_call" | custom-call | tf_op jit(solution)/shard_map/finish/pallas_call | solution.py:357
